TPU v7x, 32 devices: a whole 2x2x4 slice. The times are simulated.
32 devices in a mesh: sec: 2 (over y), row: 4 (over x, core), col: 4 (over z).
Axes of the slice: x: 2, y: 2, z: 4, core: 2. Of those that a mesh axis runs over, the one named last changes fastest.
Arguments:
- sketch: float32 [32, 64, 2048], P(None, ('sec', 'row'), 'col'), parts along dimension 1, may hold values from -6 to 6
- weights: float32 [8, 64, 2048], P(None, ('sec', 'row'), 'col'), parts along dimension 1, may hold values from 0.05 to 1
Outputs:
- basis: float32 [32, 64, 2048], P(None, ('sec', 'row'), 'col'), parts along dimension 1
- factor: float32 [64, 32], P('sec'), parts along dimension 0
There are 2 independent parts, one for each index of `sec`. A program takes and returns all parts, laid end to end along the dimension named above; each array names one. Nothing has to cross between parts.
All inputs are finite; a program needn't handle non-finite values.
Results may differ from a plain program's by a relative error of at most 0.0001.
Values sent between devices are 32-bit elements; how exact they have to be, the bound alone decides.
A program may use at most 64 MiB of HBM per device.

v0:
```python
import jax
import jax.numpy as jnp
from jax import lax
from jax.sharding import PartitionSpec as P

ITERS = 2
NEIGHBOURS = ((-1, -1), (-1, 0), (-1, 1), (0, -1), (0, 1), (1, -1), (1, 0), (1, 1))


def padded_2(block, sides, width):
    for axis, dim in sides:
        count = lax.axis_size(axis)
        forward = [(i, i + 1) for i in range(count - 1)]
        backward = [(target, source) for source, target in forward]
        low = lax.ppermute(
            lax.slice_in_dim(block, block.shape[dim] - width, None, axis=dim), axis, forward
        )
        high = lax.ppermute(lax.slice_in_dim(block, 0, width, axis=dim), axis, backward)
        block = jnp.concatenate([low, block, high], axis=dim)
    return block


def stencil(padded, local_weights):
    height = local_weights.shape[1]
    breadth = local_weights.shape[2]
    centre = padded[:, 1 : 1 + height, 1 : 1 + breadth]
    summed = jnp.sum(local_weights, axis=0) * centre
    for position, offset in enumerate(NEIGHBOURS):
        shift_row = offset[0]
        shift_col = offset[1]
        summed = (
            summed
            + local_weights[position]
            * padded[
                :, 1 + shift_row : 1 + shift_row + height, 1 + shift_col : 1 + shift_col + breadth
            ]
        )
    return summed


def factorize(interior, pixel_count):
    columns = interior.shape[0]
    flattened = interior.reshape(columns, -1)
    gram_local = jnp.dot(flattened, flattened.T, precision=lax.Precision.HIGHEST) / pixel_count
    summed = lax.psum(gram_local, ("row", "col"))
    return jnp.linalg.cholesky(summed)


def solve_planes(lower_tri, image_vals):
    columns = image_vals.shape[0]
    solved = jax.scipy.linalg.solve_triangular(
        lower_tri, image_vals.reshape(columns, -1), lower=True
    )
    return solved.reshape(image_vals.shape)


def on_device(sketch, weights):
    tile_rows = sketch.shape[1]
    tile_cols = sketch.shape[2]
    pixel_count = tile_rows * tile_cols * lax.axis_size("row") * lax.axis_size("col")
    wide_weights = padded_2(weights, (("row", 1), ("col", 2)), ITERS - 1)
    sketch_field = padded_2(sketch, (("row", 1), ("col", 2)), ITERS)
    for power_step in range(ITERS):
        margin = ITERS - 1 - power_step
        local_weights = wide_weights[
            :,
            power_step : power_step + tile_rows + 2 * margin,
            power_step : power_step + tile_cols + 2 * margin,
        ]
        image_vals = stencil(sketch_field, local_weights)
        interior = image_vals[:, margin : margin + tile_rows, margin : margin + tile_cols]
        lower_tri = factorize(interior, pixel_count)
        sketch_field = solve_planes(lower_tri, image_vals)
    return (sketch_field, lower_tri.T)


def solution(mesh):
    return jax.shard_map(
        on_device,
        mesh=mesh,
        in_specs=(P(None, ("sec", "row"), "col"), P(None, ("sec", "row"), "col")),
        out_specs=(P(None, ("sec", "row"), "col"), P("sec", None)),
        check_vma=False,
    )
```

profile of v0, /device:TPU:0, one launch (start us, length us, event | category | flops | bytes accessed | tf_op | source)
XLA Modules:
  0.0 178.7 jit_solution(1603129696953447877)
XLA Ops:
  0.6 1.1 fusion.45
  1.7 2.4 %collective-permute-start = (f32[8,1,512]{2,1,0:T(1,128)S(1)}, f32[8,1,512]{2,1,0:T(1,128)S(1)}, u32[]{:S(2)}, u32[]{:S(2)}) collective-permute-start(f32[8,1,512]{2,1,0:T(1,128)S(1)} %get-tuple-element.31), channel_id=1, source_target_pairs={{0,4},{4,8},{8,12},{1,5},{5,9},{9,13},{2,6},{6,10},{10,14},{3,7},{... | collective-permute-start | bytes 49160 | tf_op jit(solution)/shard_map/ppermute | solution.py:15
  4.1 1.4 collective-permute-start.1
  5.5 1.4 fusion.44
  6.9 5.1 %collective-permute-start.4 = (f32[32,2,512]{2,0,1:T(8,128)S(1)}, f32[32,2,512]{2,0,1:T(8,128)S(1)}, u32[]{:S(2)}, u32[]{:S(2)}) collective-permute-start(f32[32,2,512]{2,0,1:T(8,128)S(1)} %copy.47), channel_id=1, source_target_pairs={{0,4},{4,8},{8,12},{1,5},{5,9},{9,13},{2,6},{6,10},{10,14},{3,7},{... | collective-permute-start | bytes 393224 | tf_op jit(solution)/shard_map/ppermute | solution.py:15
  12.1 1.3 collective-permute-start.5
  14.3 3.5 %collective-permute-start.2 = (f32[8,10,1]{2,1,0:T(8,128)S(1)}, f32[8,10,1]{2,1,0:T(8,128)S(1)}, u32[]{:S(2)}, u32[]{:S(2)}) collective-permute-start(f32[8,10,1]{2,1,0:T(8,128)S(1)} %get-tuple-element.21), channel_id=1, source_target_pairs={{0,1},{1,2},{2,3},{4,5},{5,6},{6,7},{8,9},{9,10},{10,11},{12,13},{... | collective-permute-start | bytes 968 | tf_op jit(solution)/shard_map/ppermute | solution.py:15
  17.8 1.3 collective-permute-start.3
  19.7 4.3 %collective-permute-done.3 = f32[8,10,1]{2,1,0:T(8,128)S(1)} collective-permute-done((f32[8,10,1]{2,1,0:T(8,128)S(1)}, f32[8,10,1]{2,1,0:T(8,128)S(1)}, u32[]{:S(2)}, u32[]{:S(2)}) %collective-permute-start.3) | collective-permute-done | bytes 352 | tf_op jit(solution)/shard_map/ppermute | solution.py:18
  24.8 3.5 %collective-permute-start.6 = (f32[32,12,2]{2,0,1:T(8,128)S(1)}, f32[32,12,2]{2,0,1:T(8,128)S(1)}, u32[]{:S(2)}, u32[]{:S(2)}) collective-permute-start(f32[32,12,2]{2,0,1:T(8,128)S(1)} %get-tuple-element.7), channel_id=1, source_target_pairs={{0,1},{1,2},{2,3},{4,5},{5,6},{6,7},{8,9},{9,10},{10,11},{12,13},{... | collective-permute-start | bytes 9224 | tf_op jit(solution)/shard_map/ppermute | solution.py:15
  28.3 1.3 collective-permute-start.7
  29.6 3.9 %collective-permute-done.6 = f32[32,12,2]{2,0,1:T(8,128)S(1)} collective-permute-done((f32[32,12,2]{2,0,1:T(8,128)S(1)}, f32[32,12,2]{2,0,1:T(8,128)S(1)}, u32[]{:S(2)}, u32[]{:S(2)}) %collective-permute-start.6) | collective-permute-done | bytes 3104 | tf_op jit(solution)/shard_map/ppermute | solution.py:15
  33.5 4.1 %collective-permute-done.7 = f32[32,12,2]{2,0,1:T(8,128)S(1)} collective-permute-done((f32[32,12,2]{2,0,1:T(8,128)S(1)}, f32[32,12,2]{2,0,1:T(8,128)S(1)}, u32[]{:S(2)}, u32[]{:S(2)}) %collective-permute-start.7) | collective-permute-done | bytes 3104 | tf_op jit(solution)/shard_map/ppermute | solution.py:18
  38.0 1.4 fusion.7
  40.6 59.4 %psum.14 = f32[32,32]{0,1:T(8,128)S(1)} all-reduce(f32[32,32]{0,1:T(8,128)S(1)} %fusion.1), channel_id=1, replica_groups=mesh['sec'=2,'row'=4,'col'=4] {'row','col'}, use_global_device_ids=true, to_apply=%region_2.3 | all-reduce | flops 1024 | bytes 8192 | tf_op jit(solution)/shard_map/psum | solution.py:45
  100.1 2.9 %cholesky.44 = f32[32,32]{1,0:T(8,128)S(1)} custom-call(f32[32,32]{1,0:T(8,128)S(1)} %fusion.38), custom_call_target="Cholesky" | custom-call | tf_op jit(solution)/shard_map/jit(cholesky)/cholesky | solution.py:46
  104.4 2.4 %custom-call.10 = f32[1,32,32]{1,2,0:T(8,128)S(1)} custom-call(f32[1,32,32]{2,1,0:T(8,128)S(1)} %fusion.34), custom_call_target="InvertDiagBlocksLowerTriangular" | custom-call | tf_op jit(solution)/shard_map/jit(_solve_triangular)/triangular_solve | solution.py:51
  107.7 1.0 fusion.20
  108.7 2.1 %fusion = f32[32,32]{0,1:T(8,128)S(1)} fusion(f32[32,10,514]{2,0,1:T(8,128)S(1)} %fusion.20, f32[8,512]{1,0:T(8,128)S(1)} %get-tuple-element.29, f32[8,512]{1,0:T(8,128)S(1)} %get-tuple-element.30, f32[8,512]{1,0:T(8,128)S(1)} %get-tuple-element.24, f32[8,512]{1,0:T(8,128)S(1)} %get-tuple-element.25, f32[8,512]{1,0:T(8,128)S(1)} %get-tuple-element.26, ...), kind=kOutput, calls=%fused_computation.5 | convolution fusion | flops 54789120 | bytes 9736192 | tf_op jit(solution)/shard_map/dot_general | solution.py:44
  110.8 58.0 %psum.15 = f32[32,32]{0,1:T(8,128)S(1)} all-reduce(f32[32,32]{0,1:T(8,128)S(1)} %fusion), channel_id=1, replica_groups=mesh['sec'=2,'row'=4,'col'=4] {'row','col'}, use_global_device_ids=true, to_apply=%region_5.7 | all-reduce | flops 1024 | bytes 8192 | tf_op jit(solution)/shard_map/psum | solution.py:45
  168.8 2.9 %cholesky.55 = f32[32,32]{1,0:T(8,128)S(1)} custom-call(f32[32,32]{1,0:T(8,128)S(1)} %fusion.37), custom_call_target="Cholesky" | custom-call | tf_op jit(solution)/shard_map/jit(cholesky)/cholesky | solution.py:46
  173.0 2.4 %custom-call.11 = f32[1,32,32]{1,2,0:T(8,128)S(1)} custom-call(f32[1,32,32]{2,1,0:T(8,128)S(1)} %get-tuple-element.34), custom_call_target="InvertDiagBlocksLowerTriangular" | custom-call | tf_op jit(solution)/shard_map/jit(_solve_triangular)/triangular_solve | solution.py:51
  175.5 1.4 fusion.22
  176.9 1.1 copy.28
  (36 shorter events, 8.2 us)
Async XLA Ops:
  0.6 18.5 %copy-start = (f32[8,8,512]{2,1,0:T(8,128)S(1)}, f32[8,8,512]{2,1,0:T(8,128)}, u32[]{:S(2)}) copy-start(f32[8,8,512]{2,1,0:T(8,128)} %param.4) | copy-start | bytes 393220
  1.7 11.7 %collective-permute-start = (f32[8,1,512]{2,1,0:T(1,128)S(1)}, f32[8,1,512]{2,1,0:T(1,128)S(1)}, u32[]{:S(2)}, u32[]{:S(2)}) collective-permute-start(f32[8,1,512]{2,1,0:T(1,128)S(1)} %get-tuple-element.31), channel_id=1, source_target_pairs={{0,4},{4,8},{8,12},{1,5},{5,9},{9,13},{2,6},{6,10},{10,14},{3,7},{... | collective-permute-start | bytes 49160 | tf_op jit(solution)/shard_map/ppermute | solution.py:15
  4.1 20.2 %copy-start.1 = (f32[32,8,512]{2,1,0:T(8,128)S(1)}, f32[32,8,512]{2,1,0:T(8,128)}, u32[]{:S(2)}) copy-start(f32[32,8,512]{2,1,0:T(8,128)} %param.3) | copy-start | bytes 1572868
  4.1 9.3 %collective-permute-start.1 = (f32[8,1,512]{2,1,0:T(1,128)S(1)}, f32[8,1,512]{2,1,0:T(1,128)S(1)}, u32[]{:S(2)}, u32[]{:S(2)}) collective-permute-start(f32[8,1,512]{2,1,0:T(1,128)S(1)} %get-tuple-element.32), channel_id=1, source_target_pairs={{4,0},{8,4},{12,8},{5,1},{9,5},{13,9},{6,2},{10,6},{14,10},{7,3},{... | collective-permute-start | bytes 49160 | tf_op jit(solution)/shard_map/ppermute | solution.py:18
  6.9 17.3 %collective-permute-start.4 = (f32[32,2,512]{2,0,1:T(8,128)S(1)}, f32[32,2,512]{2,0,1:T(8,128)S(1)}, u32[]{:S(2)}, u32[]{:S(2)}) collective-permute-start(f32[32,2,512]{2,0,1:T(8,128)S(1)} %copy.47), channel_id=1, source_target_pairs={{0,4},{4,8},{8,12},{1,5},{5,9},{9,13},{2,6},{6,10},{10,14},{3,7},{... | collective-permute-start | bytes 393224 | tf_op jit(solution)/shard_map/ppermute | solution.py:15
  12.1 12.5 %collective-permute-start.5 = (f32[32,2,512]{2,0,1:T(8,128)S(1)}, f32[32,2,512]{2,0,1:T(8,128)S(1)}, u32[]{:S(2)}, u32[]{:S(2)}) collective-permute-start(f32[32,2,512]{2,0,1:T(8,128)S(1)} %copy.48), channel_id=1, source_target_pairs={{4,0},{8,4},{12,8},{5,1},{9,5},{13,9},{6,2},{10,6},{14,10},{7,3},{... | collective-permute-start | bytes 393224 | tf_op jit(solution)/shard_map/ppermute | solution.py:18
  14.3 5.4 %collective-permute-start.2 = (f32[8,10,1]{2,1,0:T(8,128)S(1)}, f32[8,10,1]{2,1,0:T(8,128)S(1)}, u32[]{:S(2)}, u32[]{:S(2)}) collective-permute-start(f32[8,10,1]{2,1,0:T(8,128)S(1)} %get-tuple-element.21), channel_id=1, source_target_pairs={{0,1},{1,2},{2,3},{4,5},{5,6},{6,7},{8,9},{9,10},{10,11},{12,13},{... | collective-permute-start | bytes 968 | tf_op jit(solution)/shard_map/ppermute | solution.py:15
  17.8 6.2 %collective-permute-start.3 = (f32[8,10,1]{2,1,0:T(8,128)S(1)}, f32[8,10,1]{2,1,0:T(8,128)S(1)}, u32[]{:S(2)}, u32[]{:S(2)}) collective-permute-start(f32[8,10,1]{2,1,0:T(8,128)S(1)} %get-tuple-element.22), channel_id=1, source_target_pairs={{1,0},{2,1},{3,2},{5,4},{6,5},{7,6},{9,8},{10,9},{11,10},{13,12},{... | collective-permute-start | bytes 968 | tf_op jit(solution)/shard_map/ppermute | solution.py:18
  24.8 8.8 %collective-permute-start.6 = (f32[32,12,2]{2,0,1:T(8,128)S(1)}, f32[32,12,2]{2,0,1:T(8,128)S(1)}, u32[]{:S(2)}, u32[]{:S(2)}) collective-permute-start(f32[32,12,2]{2,0,1:T(8,128)S(1)} %get-tuple-element.7), channel_id=1, source_target_pairs={{0,1},{1,2},{2,3},{4,5},{5,6},{6,7},{8,9},{9,10},{10,11},{12,13},{... | collective-permute-start | bytes 9224 | tf_op jit(solution)/shard_map/ppermute | solution.py:15
  28.3 9.3 %collective-permute-start.7 = (f32[32,12,2]{2,0,1:T(8,128)S(1)}, f32[32,12,2]{2,0,1:T(8,128)S(1)}, u32[]{:S(2)}, u32[]{:S(2)}) collective-permute-start(f32[32,12,2]{2,0,1:T(8,128)S(1)} %get-tuple-element.8), channel_id=1, source_target_pairs={{1,0},{2,1},{3,2},{5,4},{6,5},{7,6},{9,8},{10,9},{11,10},{13,12},{... | collective-permute-start | bytes 9224 | tf_op jit(solution)/shard_map/ppermute | solution.py:18
where the time goes:
time: 179 us
  blocking collectives  117 us (65%)
  starting transfers between devices  19.8 us (11%)
  other arithmetic  16.3 us (9%)
  waiting for transfers between devices  12.8 us (7%)
  local copies, waits for them, and re-layouts  6.29 us (4%)
  matrix products  5.25 us (3%)
    psum x2, blocking collectives, factorize(): summed = lax.psum(gram_local, ('row', 'col'))  117 us
    ppermute x4, starting transfers between devices, padded_2(): lax.ppermute(lax.slice_in_dim(block, block.shape[dim] - width, None, axis...  14.5 us
    ppermute x4, waiting for transfers between devices, padded_2(): lax.ppermute(lax.slice_in_dim(block, 0, width, axis=dim), axis, backward)  8.38 us
    another operation x6, other arithmetic, factorize(): return jnp.linalg.cholesky(summed)  7.19 us
    another operation x3, other arithmetic, solve_planes(): jax.scipy.linalg.solve_triangular(lower_tri, image_vals.reshape(columns,...  5.52 us
    ppermute x4, starting transfers between devices, padded_2(): lax.ppermute(lax.slice_in_dim(block, 0, width, axis=dim), axis, backward)  5.3 us
    ppermute x4, waiting for transfers between devices, padded_2(): lax.ppermute(lax.slice_in_dim(block, block.shape[dim] - width, None, axis...  4.46 us
  transfers between devices with their start and end apart: 8, of which 4 were waited for; matrix products, arithmetic and copies ran while one was open for 2% of the time, Pallas kernels for 0%

commit v1 on v0

--- a/solution.py
+++ b/solution.py
@@ -42,7 +42,7 @@
     columns = interior.shape[0]
     flattened = interior.reshape(columns, -1)
     gram_local = jnp.dot(flattened, flattened.T, precision=lax.Precision.HIGHEST) / pixel_count
-    summed = lax.psum(gram_local, ("row", "col"))
+    summed = lax.psum(lax.psum(gram_local, "col"), "row")
     return jnp.linalg.cholesky(summed)
 
 

time: 179 us -> 115 us (0.64)
  blocking collectives: 117 us -> 52.9 us
    psum x2 -> x4, blocking collectives: 117 us -> 52.9 us  [factorize(): summed = lax.psum(lax.psum(gram_local, 'col'), 'row')]
  transfers between devices with their start and end apart: 8 -> 8, of which waited for: 4 -> 4; matrix products, arithmetic and copies ran while one was open for 2% -> 3% of each run, Pallas kernels for 0% -> 0%
where the time goes in v1:
time: 115 us; the launch traced here: 114 us
  blocking collectives  52.9 us (46%)
  starting transfers between devices  19.8 us (17%)
  other arithmetic  16.3 us (14%)
  waiting for transfers between devices  12.8 us (11%)
  local copies, waits for them, and re-layouts  6.3 us (5%)
  matrix products  5.25 us (5%)
    psum x4, blocking collectives, factorize(): summed = lax.psum(lax.psum(gram_local, 'col'), 'row')  52.9 us
    ppermute x4, starting transfers between devices, padded_2(): lax.ppermute(lax.slice_in_dim(block, block.shape[dim] - width, None, axis...  14.5 us
    ppermute x4, waiting for transfers between devices, padded_2(): lax.ppermute(lax.slice_in_dim(block, 0, width, axis=dim), axis, backward)  8.38 us
    another operation x6, other arithmetic, factorize(): return jnp.linalg.cholesky(summed)  7.19 us
    another operation x3, other arithmetic, solve_planes(): jax.scipy.linalg.solve_triangular(lower_tri, image_vals.reshape(columns,...  5.52 us
    ppermute x4, starting transfers between devices, padded_2(): lax.ppermute(lax.slice_in_dim(block, 0, width, axis=dim), axis, backward)  5.3 us
    ppermute x4, waiting for transfers between devices, padded_2(): lax.ppermute(lax.slice_in_dim(block, block.shape[dim] - width, None, axis...  4.46 us
    dot_general x2, matrix products, factorize(): jnp.dot(flattened, flattened.T, precision=lax.Precision.HIGHEST)  2.82 us
  transfers between devices with their start and end apart: 8, of which 4 were waited for; matrix products, arithmetic and copies ran while one was open for 3% of the time, Pallas kernels for 0%

profile of v1, /device:TPU:0, one launch (start us, length us, event | category | flops | bytes accessed | tf_op | source)
XLA Modules:
  0.0 114.3 jit_solution(15108318546375269612)
XLA Ops:
  1.7 2.4 %collective-permute-start = (f32[8,1,512]{2,1,0:T(1,128)S(1)}, f32[8,1,512]{2,1,0:T(1,128)S(1)}, u32[]{:S(2)}, u32[]{:S(2)}) collective-permute-start(f32[8,1,512]{2,1,0:T(1,128)S(1)} %get-tuple-element.31), channel_id=1, source_target_pairs={{0,4},{4,8},{8,12},{1,5},{5,9},{9,13},{2,6},{6,10},{10,14},{3,7},{... | collective-permute-start | bytes 49160 | tf_op jit(solution)/shard_map/ppermute | solution.py:15
  4.1 1.4 %collective-permute-start.1 = (f32[8,1,512]{2,1,0:T(1,128)S(1)}, f32[8,1,512]{2,1,0:T(1,128)S(1)}, u32[]{:S(2)}, u32[]{:S(2)}) collective-permute-start(f32[8,1,512]{2,1,0:T(1,128)S(1)} %get-tuple-element.32), channel_id=1, source_target_pairs={{4,0},{8,4},{12,8},{5,1},{9,5},{13,9},{6,2},{10,6},{14,10},{7,3},{... | collective-permute-start | bytes 49160 | tf_op jit(solution)/shard_map/ppermute | solution.py:18
  5.5 1.4 %fusion.44 = (f32[32,2,512]{2,1,0:T(2,128)S(1)}, f32[32,2,512]{2,1,0:T(2,128)S(1)}) fusion(f32[32,8,512]{2,1,0:T(8,128)} %param.3), kind=kLoop, calls=%fused_computation.102 | loop fusion | bytes 524288 | tf_op jit(solution)/shard_map/slice | solution.py:18
  6.9 5.1 %collective-permute-start.4 = (f32[32,2,512]{2,0,1:T(8,128)S(1)}, f32[32,2,512]{2,0,1:T(8,128)S(1)}, u32[]{:S(2)}, u32[]{:S(2)}) collective-permute-start(f32[32,2,512]{2,0,1:T(8,128)S(1)} %copy.47), channel_id=1, source_target_pairs={{0,4},{4,8},{8,12},{1,5},{5,9},{9,13},{2,6},{6,10},{10,14},{3,7},{... | collective-permute-start | bytes 393224 | tf_op jit(solution)/shard_map/ppermute | solution.py:15
  12.1 1.3 %collective-permute-start.5 = (f32[32,2,512]{2,0,1:T(8,128)S(1)}, f32[32,2,512]{2,0,1:T(8,128)S(1)}, u32[]{:S(2)}, u32[]{:S(2)}) collective-permute-start(f32[32,2,512]{2,0,1:T(8,128)S(1)} %copy.48), channel_id=1, source_target_pairs={{4,0},{8,4},{12,8},{5,1},{9,5},{13,9},{6,2},{10,6},{14,10},{7,3},{... | collective-permute-start | bytes 393224 | tf_op jit(solution)/shard_map/ppermute | solution.py:18
  14.3 3.5 %collective-permute-start.2 = (f32[8,10,1]{2,1,0:T(8,128)S(1)}, f32[8,10,1]{2,1,0:T(8,128)S(1)}, u32[]{:S(2)}, u32[]{:S(2)}) collective-permute-start(f32[8,10,1]{2,1,0:T(8,128)S(1)} %get-tuple-element.21), channel_id=1, source_target_pairs={{0,1},{1,2},{2,3},{4,5},{5,6},{6,7},{8,9},{9,10},{10,11},{12,13},{... | collective-permute-start | bytes 968 | tf_op jit(solution)/shard_map/ppermute | solution.py:15
  17.8 1.3 %collective-permute-start.3 = (f32[8,10,1]{2,1,0:T(8,128)S(1)}, f32[8,10,1]{2,1,0:T(8,128)S(1)}, u32[]{:S(2)}, u32[]{:S(2)}) collective-permute-start(f32[8,10,1]{2,1,0:T(8,128)S(1)} %get-tuple-element.22), channel_id=1, source_target_pairs={{1,0},{2,1},{3,2},{5,4},{6,5},{7,6},{9,8},{10,9},{11,10},{13,12},{... | collective-permute-start | bytes 968 | tf_op jit(solution)/shard_map/ppermute | solution.py:18
  19.7 4.3 %collective-permute-done.3 = f32[8,10,1]{2,1,0:T(8,128)S(1)} collective-permute-done((f32[8,10,1]{2,1,0:T(8,128)S(1)}, f32[8,10,1]{2,1,0:T(8,128)S(1)}, u32[]{:S(2)}, u32[]{:S(2)}) %collective-permute-start.3) | collective-permute-done | bytes 352 | tf_op jit(solution)/shard_map/ppermute | solution.py:18
  24.8 3.5 %collective-permute-start.6 = (f32[32,12,2]{2,0,1:T(8,128)S(1)}, f32[32,12,2]{2,0,1:T(8,128)S(1)}, u32[]{:S(2)}, u32[]{:S(2)}) collective-permute-start(f32[32,12,2]{2,0,1:T(8,128)S(1)} %get-tuple-element.7), channel_id=1, source_target_pairs={{0,1},{1,2},{2,3},{4,5},{5,6},{6,7},{8,9},{9,10},{10,11},{12,13},{... | collective-permute-start | bytes 9224 | tf_op jit(solution)/shard_map/ppermute | solution.py:15
  28.3 1.3 %collective-permute-start.7 = (f32[32,12,2]{2,0,1:T(8,128)S(1)}, f32[32,12,2]{2,0,1:T(8,128)S(1)}, u32[]{:S(2)}, u32[]{:S(2)}) collective-permute-start(f32[32,12,2]{2,0,1:T(8,128)S(1)} %get-tuple-element.8), channel_id=1, source_target_pairs={{1,0},{2,1},{3,2},{5,4},{6,5},{7,6},{9,8},{10,9},{11,10},{13,12},{... | collective-permute-start | bytes 9224 | tf_op jit(solution)/shard_map/ppermute | solution.py:18
  29.6 3.9 %collective-permute-done.6 = f32[32,12,2]{2,0,1:T(8,128)S(1)} collective-permute-done((f32[32,12,2]{2,0,1:T(8,128)S(1)}, f32[32,12,2]{2,0,1:T(8,128)S(1)}, u32[]{:S(2)}, u32[]{:S(2)}) %collective-permute-start.6) | collective-permute-done | bytes 3104 | tf_op jit(solution)/shard_map/ppermute | solution.py:15
  33.5 4.1 %collective-permute-done.7 = f32[32,12,2]{2,0,1:T(8,128)S(1)} collective-permute-done((f32[32,12,2]{2,0,1:T(8,128)S(1)}, f32[32,12,2]{2,0,1:T(8,128)S(1)}, u32[]{:S(2)}, u32[]{:S(2)}) %collective-permute-start.7) | collective-permute-done | bytes 3104 | tf_op jit(solution)/shard_map/ppermute | solution.py:18
  38.0 1.4 %fusion.7 = f32[32,10,514]{2,0,1:T(8,128)S(1)} fusion(f32[32,12,512]{2,0,1:T(8,128)S(1)} %constant_dynamic-update-slice_fusion, f32[32,12,2]{2,0,1:T(8,128)S(1)} %collective-permute-done.7, f32[32,12,2]{2,0,1:T(8,128)S(1)} %collective-permute-done.6, f32[32,12,516]{2,0,1:T(8,128)S(1)} %pad_maximum_fusion, f32[10,514]{1,0:T(8,128)S(1)} %get-tuple-element.18, ...), kind=kLoop, calls=%fused_computation.18 | loop fusion | flops 3783040 | bytes 3609296 | tf_op jit(solution)/shard_map/add | solution.py:32
  40.6 17.0 %psum.28 = f32[32,32]{0,1:T(8,128)S(1)} all-reduce(f32[32,32]{0,1:T(8,128)S(1)} %fusion.1), channel_id=1, replica_groups=mesh['sec'=2,'row'=4,'col'=4] {'col'}, use_global_device_ids=true, to_apply=%region_2.0 | all-reduce | flops 1024 | bytes 8192 | tf_op jit(solution)/shard_map/psum | solution.py:45
  57.6 10.1 %psum.29 = f32[32,32]{0,1:T(8,128)S(1)} all-reduce(f32[32,32]{0,1:T(8,128)S(1)} %psum.28), channel_id=1, replica_groups=mesh['sec'=2,'row'=4,'col'=4] {'row'}, use_global_device_ids=true, to_apply=%region_3.4 | all-reduce | flops 1024 | bytes 8192 | tf_op jit(solution)/shard_map/psum | solution.py:45
  67.8 2.9 %cholesky.44 = f32[32,32]{1,0:T(8,128)S(1)} custom-call(f32[32,32]{1,0:T(8,128)S(1)} %fusion.38), custom_call_target="Cholesky" | custom-call | tf_op jit(solution)/shard_map/jit(cholesky)/cholesky | solution.py:46
  72.1 2.4 %custom-call.10 = f32[1,32,32]{1,2,0:T(8,128)S(1)} custom-call(f32[1,32,32]{2,1,0:T(8,128)S(1)} %fusion.34), custom_call_target="InvertDiagBlocksLowerTriangular" | custom-call | tf_op jit(solution)/shard_map/jit(_solve_triangular)/triangular_solve | solution.py:51
  76.4 2.1 %fusion = f32[32,32]{0,1:T(8,128)S(1)} fusion(f32[32,10,514]{2,0,1:T(8,128)S(1)} %fusion.20, f32[8,512]{1,0:T(8,128)S(1)} %get-tuple-element.29, f32[8,512]{1,0:T(8,128)S(1)} %get-tuple-element.30, f32[8,512]{1,0:T(8,128)S(1)} %get-tuple-element.24, f32[8,512]{1,0:T(8,128)S(1)} %get-tuple-element.25, f32[8,512]{1,0:T(8,128)S(1)} %get-tuple-element.26, ...), kind=kOutput, calls=%fused_computation.5 | convolution fusion | flops 54789120 | bytes 9736192 | tf_op jit(solution)/shard_map/dot_general | solution.py:44
  78.5 15.5 %psum.30 = f32[32,32]{0,1:T(8,128)S(1)} all-reduce(f32[32,32]{0,1:T(8,128)S(1)} %fusion), channel_id=1, replica_groups=mesh['sec'=2,'row'=4,'col'=4] {'col'}, use_global_device_ids=true, to_apply=%region_6.8 | all-reduce | flops 1024 | bytes 8192 | tf_op jit(solution)/shard_map/psum | solution.py:45
  94.0 10.3 %psum.31 = f32[32,32]{0,1:T(8,128)S(1)} all-reduce(f32[32,32]{0,1:T(8,128)S(1)} %psum.30), channel_id=1, replica_groups=mesh['sec'=2,'row'=4,'col'=4] {'row'}, use_global_device_ids=true, to_apply=%region_7.9 | all-reduce | flops 1024 | bytes 8192 | tf_op jit(solution)/shard_map/psum | solution.py:45
  104.4 2.9 %cholesky.55 = f32[32,32]{1,0:T(8,128)S(1)} custom-call(f32[32,32]{1,0:T(8,128)S(1)} %fusion.37), custom_call_target="Cholesky" | custom-call | tf_op jit(solution)/shard_map/jit(cholesky)/cholesky | solution.py:46
  108.6 2.4 %custom-call.11 = f32[1,32,32]{1,2,0:T(8,128)S(1)} custom-call(f32[1,32,32]{2,1,0:T(8,128)S(1)} %get-tuple-element.34), custom_call_target="InvertDiagBlocksLowerTriangular" | custom-call | tf_op jit(solution)/shard_map/jit(_solve_triangular)/triangular_solve | solution.py:51
  111.1 1.4 %fusion.22 = f32[32,8,512]{2,0,1:T(8,128)S(1)} fusion(f32[1,32,32]{1,2,0:T(8,128)S(1)} %custom-call.11, f32[32,10,514]{2,0,1:T(8,128)S(1)} %fusion.20, f32[8,512]{1,0:T(8,128)S(1)} %get-tuple-element.29, f32[8,512]{1,0:T(8,128)S(1)} %get-tuple-element.30, f32[8,512]{1,0:T(8,128)S(1)} %get-tuple-element.24, f32[8,512]{1,0:T(8,128)S(1)} %get-tuple-element.25, ...), kind=kOutput, calls=%fused_computation.38 | convolution fusion | flops 52559872 | bytes 5406720 | tf_op jit(solution)/shard_map/jit(_solve_triangular)/triangular_solve | solution.py:51
  112.5 1.1 copy.28
  (38 shorter events, 10.3 us)
Async XLA Ops:
  0.6 18.5 %copy-start = (f32[8,8,512]{2,1,0:T(8,128)S(1)}, f32[8,8,512]{2,1,0:T(8,128)}, u32[]{:S(2)}) copy-start(f32[8,8,512]{2,1,0:T(8,128)} %param.4) | copy-start | bytes 393220
  1.7 11.7 %collective-permute-start = (f32[8,1,512]{2,1,0:T(1,128)S(1)}, f32[8,1,512]{2,1,0:T(1,128)S(1)}, u32[]{:S(2)}, u32[]{:S(2)}) collective-permute-start(f32[8,1,512]{2,1,0:T(1,128)S(1)} %get-tuple-element.31), channel_id=1, source_target_pairs={{0,4},{4,8},{8,12},{1,5},{5,9},{9,13},{2,6},{6,10},{10,14},{3,7},{... | collective-permute-start | bytes 49160 | tf_op jit(solution)/shard_map/ppermute | solution.py:15
  4.1 20.2 %copy-start.1 = (f32[32,8,512]{2,1,0:T(8,128)S(1)}, f32[32,8,512]{2,1,0:T(8,128)}, u32[]{:S(2)}) copy-start(f32[32,8,512]{2,1,0:T(8,128)} %param.3) | copy-start | bytes 1572868
  4.1 9.3 %collective-permute-start.1 = (f32[8,1,512]{2,1,0:T(1,128)S(1)}, f32[8,1,512]{2,1,0:T(1,128)S(1)}, u32[]{:S(2)}, u32[]{:S(2)}) collective-permute-start(f32[8,1,512]{2,1,0:T(1,128)S(1)} %get-tuple-element.32), channel_id=1, source_target_pairs={{4,0},{8,4},{12,8},{5,1},{9,5},{13,9},{6,2},{10,6},{14,10},{7,3},{... | collective-permute-start | bytes 49160 | tf_op jit(solution)/shard_map/ppermute | solution.py:18
  6.9 17.3 %collective-permute-start.4 = (f32[32,2,512]{2,0,1:T(8,128)S(1)}, f32[32,2,512]{2,0,1:T(8,128)S(1)}, u32[]{:S(2)}, u32[]{:S(2)}) collective-permute-start(f32[32,2,512]{2,0,1:T(8,128)S(1)} %copy.47), channel_id=1, source_target_pairs={{0,4},{4,8},{8,12},{1,5},{5,9},{9,13},{2,6},{6,10},{10,14},{3,7},{... | collective-permute-start | bytes 393224 | tf_op jit(solution)/shard_map/ppermute | solution.py:15
  12.1 12.5 %collective-permute-start.5 = (f32[32,2,512]{2,0,1:T(8,128)S(1)}, f32[32,2,512]{2,0,1:T(8,128)S(1)}, u32[]{:S(2)}, u32[]{:S(2)}) collective-permute-start(f32[32,2,512]{2,0,1:T(8,128)S(1)} %copy.48), channel_id=1, source_target_pairs={{4,0},{8,4},{12,8},{5,1},{9,5},{13,9},{6,2},{10,6},{14,10},{7,3},{... | collective-permute-start | bytes 393224 | tf_op jit(solution)/shard_map/ppermute | solution.py:18
  14.3 5.4 %collective-permute-start.2 = (f32[8,10,1]{2,1,0:T(8,128)S(1)}, f32[8,10,1]{2,1,0:T(8,128)S(1)}, u32[]{:S(2)}, u32[]{:S(2)}) collective-permute-start(f32[8,10,1]{2,1,0:T(8,128)S(1)} %get-tuple-element.21), channel_id=1, source_target_pairs={{0,1},{1,2},{2,3},{4,5},{5,6},{6,7},{8,9},{9,10},{10,11},{12,13},{... | collective-permute-start | bytes 968 | tf_op jit(solution)/shard_map/ppermute | solution.py:15
  17.8 6.2 %collective-permute-start.3 = (f32[8,10,1]{2,1,0:T(8,128)S(1)}, f32[8,10,1]{2,1,0:T(8,128)S(1)}, u32[]{:S(2)}, u32[]{:S(2)}) collective-permute-start(f32[8,10,1]{2,1,0:T(8,128)S(1)} %get-tuple-element.22), channel_id=1, source_target_pairs={{1,0},{2,1},{3,2},{5,4},{6,5},{7,6},{9,8},{10,9},{11,10},{13,12},{... | collective-permute-start | bytes 968 | tf_op jit(solution)/shard_map/ppermute | solution.py:18
  24.8 8.8 %collective-permute-start.6 = (f32[32,12,2]{2,0,1:T(8,128)S(1)}, f32[32,12,2]{2,0,1:T(8,128)S(1)}, u32[]{:S(2)}, u32[]{:S(2)}) collective-permute-start(f32[32,12,2]{2,0,1:T(8,128)S(1)} %get-tuple-element.7), channel_id=1, source_target_pairs={{0,1},{1,2},{2,3},{4,5},{5,6},{6,7},{8,9},{9,10},{10,11},{12,13},{... | collective-permute-start | bytes 9224 | tf_op jit(solution)/shard_map/ppermute | solution.py:15
  28.3 9.3 %collective-permute-start.7 = (f32[32,12,2]{2,0,1:T(8,128)S(1)}, f32[32,12,2]{2,0,1:T(8,128)S(1)}, u32[]{:S(2)}, u32[]{:S(2)}) collective-permute-start(f32[32,12,2]{2,0,1:T(8,128)S(1)} %get-tuple-element.8), channel_id=1, source_target_pairs={{1,0},{2,1},{3,2},{5,4},{6,5},{7,6},{9,8},{10,9},{11,10},{13,12},{... | collective-permute-start | bytes 9224 | tf_op jit(solution)/shard_map/ppermute | solution.py:18
